TPU v7x, 128 devices: a whole 4x4x4 slice. The times are simulated.
128 devices in a mesh: row: 4 (over x), col: 32 (over z, y, core).
Axes of the slice: x: 4, y: 4, z: 4, core: 2. Of those that a mesh axis runs over, the one named last changes fastest.
Arguments:
- tokens: bfloat16 [512, 8192], P('col', 'row'), may hold values from -6 to 6
- out_grad: bfloat16 [512, 8192], P('col', 'row'), may hold values from -6 to 6
- gate_weight: bfloat16 [8192, 29568], P('row', 'col'), may hold values from -0.0625 to 0.0625
- up_weight: bfloat16 [8192, 29568], P('row', 'col'), may hold values from -0.0625 to 0.0625
- down_weight: bfloat16 [29568, 8192], P('col', 'row'), may hold values from -0.03125 to 0.03125
Outputs:
- input_grad: bfloat16 [512, 8192], P('col', 'row')
- gate_wgrad: bfloat16 [8192, 29568], P('row', 'col')
- up_wgrad: bfloat16 [8192, 29568], P('row', 'col')
- down_wgrad: bfloat16 [29568, 8192], P('col', 'row')
All inputs are finite; a program needn't handle non-finite values.
Results may differ from a plain program's by a relative error of at most 0.005.
Values may be sent and summed in bfloat16 or wider, within the bound.
No kernel may reach another device: no remote copies, remote signals or barrier semaphores. Data moves between devices by JAX's collectives and lax.ppermute only.
A program may use at most 128 MiB of HBM per device.

v0:
```python
import math
import jax
import jax.numpy as jnp
from jax import lax
from jax.sharding import PartitionSpec as P


def contract(left, right, left_dim, right_dim):
    return lax.dot_general(
        left, right, (((left_dim,), (right_dim,)), ((), ())), preferred_element_type=jnp.float32
    )


def swiglu_backward(gate, upward, hid_grad):
    sig = jax.nn.sigmoid(gate)
    act = gate * sig
    hidden = (act * upward).astype(jnp.bfloat16)
    gate_grad = (hid_grad * upward * sig * (1.0 + gate * (1.0 - sig))).astype(jnp.bfloat16)
    up_grad = (hid_grad * act).astype(jnp.bfloat16)
    return (hidden, gate_grad, up_grad)


def local(tokens, out_grad, gate_weight, up_weight, down_weight):
    panel_tokens, panel_grads = (
        lax.all_gather(tokens, "col", axis=0, tiled=True),
        lax.all_gather(out_grad, "col", axis=0, tiled=True),
    )
    factor = 1.0 / math.sqrt(panel_tokens.shape[0])
    gate_part = jnp.dot(panel_tokens, gate_weight, preferred_element_type=jnp.float32)
    up_part = jnp.dot(panel_tokens, up_weight, preferred_element_type=jnp.float32)
    grad_part = contract(panel_grads, down_weight, 1, 1)
    gate, upward, hid_grad = lax.psum((gate_part, up_part, grad_part), "row")
    hidden, gate_grad, up_grad = swiglu_backward(gate, upward, hid_grad)
    input_grad = lax.psum_scatter(
        contract(gate_grad, gate_weight, 1, 1) + contract(up_grad, up_weight, 1, 1),
        "col",
        scatter_dimension=0,
        tiled=True,
    ).astype(jnp.bfloat16)
    gate_wgrad = (contract(panel_tokens, gate_grad, 0, 0) * factor).astype(jnp.bfloat16)
    up_wgrad = (contract(panel_tokens, up_grad, 0, 0) * factor).astype(jnp.bfloat16)
    down_wgrad = (contract(hidden, panel_grads, 0, 0) * factor).astype(jnp.bfloat16)
    return (input_grad, gate_wgrad, up_wgrad, down_wgrad)


def solution(mesh):
    placed = (P("col", "row"), P("col", "row"), P("row", "col"), P("row", "col"), P("col", "row"))
    return jax.shard_map(
        local,
        mesh=mesh,
        in_specs=placed,
        out_specs=(P("col", "row"), P("row", "col"), P("row", "col"), P("col", "row")),
        check_vma=False,
    )
```

profile of v0, /device:TPU:0, one launch (start us, length us, event | category | flops | bytes accessed | tf_op | source)
XLA Modules:
  0.0 326.6 jit_solution(14472059379591102396)
XLA Ops:
  7.2 0.0 all-gather.5.cloned.1.call-start
  7.2 0.7 all-gather.5.cloned.1.call-update
  7.9 0.0 all-gather.3.cloned.1.call-start
  7.9 0.7 all-gather.3.cloned.1.call-update
  8.6 0.0 all-reduce.3.cloned.1.call-start
  8.7 48.1 %all-gather.5.cloned.1.call-done = bf16[512,2048]{1,0:T(8,128)(2,1)} async-done(((bf16[16,2048]{1,0:T(8,128)(2,1)}), bf16[512,2048]{1,0:T(8,128)(2,1)}) %all-gather.5.cloned.1.call-update) | async-done | bytes 2097168 | tf_op jit(solution)/shard_map/all_gather | solution.py:25
  56.8 0.0 copy-start
  56.8 0.0 copy-start.5
  56.8 6.3 %fusion.6 = f32[512,924]{0,1:T(8,128)} fusion(bf16[512,2048]{1,0:T(8,128)(2,1)} %all-gather.5.cloned.1.call-done, bf16[2048,924]{0,1:T(8,128)(2,1)} %param.8), kind=kOutput, calls=%fused_computation.13 | convolution fusion | flops 1937768448 | bytes 7774208 | tf_op jit(solution)/shard_map/dot_general | solution.py:30
  63.0 0.0 copy-done
  63.0 0.0 copy-done.5
  63.0 3.4 %fusion.7 = f32[512,924]{0,1:T(8,128)} fusion(bf16[512,2048]{1,0:T(8,128)(2,1)S(1)} %copy-done.5, bf16[2048,924]{0,1:T(8,128)(2,1)S(1)} %copy-done), kind=kOutput, calls=%fused_computation.14 | convolution fusion | flops 1937768448 | bytes 7774208 | tf_op jit(solution)/shard_map/dot_general | solution.py:29
  66.4 35.8 %all-gather.3.cloned.1.call-done = bf16[512,2048]{1,0:T(8,128)(2,1)} async-done(((bf16[16,2048]{1,0:T(8,128)(2,1)}), bf16[512,2048]{1,0:T(8,128)(2,1)}) %all-gather.3.cloned.1.call-update) | async-done | bytes 2097168 | tf_op jit(solution)/shard_map/all_gather | solution.py:26
  102.3 6.1 %fusion.5 = f32[512,924]{0,1:T(8,128)} fusion(bf16[512,2048]{1,0:T(8,128)(2,1)} %all-gather.3.cloned.1.call-done, bf16[924,2048]{1,0:T(8,128)(2,1)} %param.9), kind=kOutput, calls=%fused_computation.12 | convolution fusion | flops 1937768448 | bytes 7774208 | tf_op jit(solution)/shard_map/dot_general | solution.py:9
  108.4 0.0 all-reduce.3.cloned.1.call-update
  108.4 0.2 reduce-scatter.2.cloned.1.call-start
  108.7 116.8 %all-reduce.3.cloned.1.call-done = (f32[512,924]{0,1:T(8,128)}, f32[512,924]{0,1:T(8,128)}, f32[512,924]{0,1:T(8,128)}) async-done(((f32[512,924]{0,1:T(8,128)}, f32[512,924]{0,1:T(8,128)}, f32[512,924]{0,1:T(8,128)}), (f32[512,924]{0,1:T(8,128)}, f32[512,924]{0,1:T(8,128)}, f32[512,924]{0,1:T(8,128)})) %all-reduce.3.cloned.1.call-update) | async-done | bytes 5677072 | tf_op jit(solution)/shard_map/psum | solution.py:32
  225.4 0.0 copy-start.1
  225.4 3.9 %multiply_convert_fusion.4 = (bf16[512,924]{0,1:T(8,128)(2,1)S(1)}, bf16[512,924]{0,1:T(8,128)(2,1)S(1)}) fusion(f32[512,924]{0,1:T(8,128)} %get-tuple-element.5, f32[512,924]{0,1:T(8,128)} %get-tuple-element.4, f32[512,924]{0,1:T(8,128)} %get-tuple-element.6), kind=kLoop, calls=%fused_computation.7 | loop fusion | flops 6150144 | bytes 7569408 | tf_op jit(solution)/shard_map/convert_element_type | solution.py:19
  229.3 0.0 copy-done.1
  229.3 0.0 copy-start.2
  229.3 2.4 fusion.8
  231.8 0.0 copy-done.2
  231.8 4.5 %convolution_add_fusion = f32[512,2048]{1,0:T(8,128)} fusion(f32[512,2048]{1,0:T(8,128)S(1)} %fusion.8, bf16[512,924]{0,1:T(8,128)(2,1)S(1)} %get-tuple-element.7, bf16[2048,924]{0,1:T(8,128)(2,1)S(1)} %copy-done.2), kind=kOutput, calls=%fused_computation.5 | convolution fusion | flops 1938817024 | bytes 13119488 | tf_op jit(solution)/shard_map/dot_general | solution.py:9
  236.3 0.0 reduce-scatter.2.cloned.1.call-update
  236.3 0.0 copy-start.6
  236.3 5.8 %fusion = bf16[2048,924]{0,1:T(8,128)(2,1)} fusion(bf16[512,924]{0,1:T(8,128)(2,1)S(1)} %get-tuple-element.8, bf16[512,2048]{1,0:T(8,128)(2,1)} %all-gather.5.cloned.1.call-done), kind=kOutput, calls=%fused_computation.3 | convolution fusion | flops 1941553152 | bytes 6828032 | tf_op jit(solution)/shard_map/dot_general | solution.py:9
  242.1 0.0 copy-done.6
  242.1 0.0 copy-start.3
  242.1 0.0 copy-start.4
  242.1 0.0 copy-start.7
  242.1 4.1 %fusion.1 = bf16[2048,924]{0,1:T(8,128)(2,1)} fusion(bf16[512,924]{0,1:T(8,128)(2,1)S(1)} %get-tuple-element.7, bf16[512,2048]{1,0:T(8,128)(2,1)S(1)} %copy-done.6), kind=kOutput, calls=%fused_computation.4 | convolution fusion | flops 1941553152 | bytes 6828032 | tf_op jit(solution)/shard_map/dot_general | solution.py:9
  246.2 0.0 copy-done.3
  246.2 0.0 copy-done.4
  246.2 0.0 copy-done.7
  246.2 4.1 %multiply_convert_fusion = bf16[924,2048]{1,0:T(8,128)(2,1)} fusion(bf16[512,2048]{1,0:T(8,128)(2,1)S(1)} %copy-done.7, f32[512,924]{0,1:T(8,128)S(1)} %copy-done.4, f32[512,924]{0,1:T(8,128)S(1)} %copy-done.3), kind=kOutput, calls=%fused_computation | convolution fusion | flops 1944391680 | bytes 9666560 | tf_op jit(solution)/shard_map/dot_general | solution.py:9
  250.3 68.2 %reduce-scatter.2.cloned.1.call-done = f32[16,2048]{1,0:T(8,128)} async-done(((f32[512,2048]{1,0:T(8,128)}), f32[16,2048]{1,0:T(8,128)}) %reduce-scatter.2.cloned.1.call-update) | async-done | bytes 131088 | tf_op jit(solution)/shard_map/reduce_scatter | solution.py:34
  318.5 1.5 convert_element_type.29
Async XLA Ops:
  7.2 49.6 %all-gather.5.cloned.1.call-start = ((), (), s32[]{:S(2)}) async-start(), calls=%async_computation.2 | async-start | bytes 2162688 | tf_op jit(solution)/shard_map/all_gather | solution.py:25
  7.9 94.4 %all-gather.3.cloned.1.call-start = ((), (), s32[]{:S(2)}) async-start(), calls=%async_computation.1 | async-start | bytes 2162688 | tf_op jit(solution)/shard_map/all_gather | solution.py:26
  8.6 216.8 %all-reduce.3.cloned.1.call-start = ((), (), s32[]{:S(2)}) async-start(), calls=%async_computation.4 | async-start | bytes 11403264 | tf_op jit(solution)/shard_map/psum | solution.py:32
  56.8 6.3 %copy-start = (bf16[2048,924]{0,1:T(8,128)(2,1)S(1)}, bf16[2048,924]{0,1:T(8,128)(2,1)}, u32[]{:S(2)}) copy-start(bf16[2048,924]{0,1:T(8,128)(2,1)} %param.7) | copy-start | bytes 11354116
  56.8 6.3 %copy-start.5 = (bf16[512,2048]{1,0:T(8,128)(2,1)S(1)}, bf16[512,2048]{1,0:T(8,128)(2,1)}, u32[]{:S(2)}) copy-start(bf16[512,2048]{1,0:T(8,128)(2,1)} %all-gather.5.cloned.1.call-done) | copy-start | bytes 6291460
  108.4 210.1 %reduce-scatter.2.cloned.1.call-start = ((), (), s32[]{:S(2)}) async-start(), calls=%async_computation.3 | async-start | bytes 4325376 | tf_op jit(solution)/shard_map/reduce_scatter | solution.py:34
  225.4 3.9 %copy-start.1 = (bf16[2048,924]{0,1:T(8,128)(2,1)S(1)}, bf16[2048,924]{0,1:T(8,128)(2,1)}, u32[]{:S(2)}) copy-start(bf16[2048,924]{0,1:T(8,128)(2,1)} %param.7) | copy-start | bytes 11354116
  229.3 2.4 copy-start.2
  236.3 5.8 %copy-start.6 = (bf16[512,2048]{1,0:T(8,128)(2,1)S(1)}, bf16[512,2048]{1,0:T(8,128)(2,1)}, u32[]{:S(2)}) copy-start(bf16[512,2048]{1,0:T(8,128)(2,1)} %all-gather.5.cloned.1.call-done) | copy-start | bytes 6291460
  242.1 4.1 %copy-start.3 = (f32[512,924]{0,1:T(8,128)S(1)}, f32[512,924]{0,1:T(8,128)}, u32[]{:S(2)}) copy-start(f32[512,924]{0,1:T(8,128)} %get-tuple-element.4) | copy-start | bytes 5677060
  242.1 4.1 %copy-start.4 = (f32[512,924]{0,1:T(8,128)S(1)}, f32[512,924]{0,1:T(8,128)}, u32[]{:S(2)}) copy-start(f32[512,924]{0,1:T(8,128)} %get-tuple-element.6) | copy-start | bytes 5677060
  242.1 4.1 %copy-start.7 = (bf16[512,2048]{1,0:T(8,128)(2,1)S(1)}, bf16[512,2048]{1,0:T(8,128)(2,1)}, u32[]{:S(2)}) copy-start(bf16[512,2048]{1,0:T(8,128)(2,1)} %all-gather.3.cloned.1.call-done) | copy-start | bytes 6291460
Sparse Core Ops, SparseCore 0:
  10.3 46.4 all-gather.4
  59.0 43.2 all-gather.2
  108.5 116.8 all-reduce.2
  236.4 81.9 reduce-scatter.1
where the time goes:
time: 327 us
  waiting for transfers between devices  270 us (83%)
  matrix products  36.7 us (11%)
  between operations  13.8 us (4%)
  other arithmetic  5.43 us (2%)
    psum x1, waiting for transfers between devices, local(): gate, upward, hid_grad = lax.psum((gate_part, up_part, grad_part), 'row')  117 us
    reduce_scatter x1, waiting for transfers between devices, local(): lax.psum_scatter(contract(gate_grad, gate_weight, 1, 1) + contract(up_gra...  68.2 us
    all_gather x1, waiting for transfers between devices, local(): lax.all_gather(tokens, 'col', axis=0, tiled=True)  48.1 us
    all_gather x1, waiting for transfers between devices, local(): lax.all_gather(out_grad, 'col', axis=0, tiled=True)  35.8 us
    dot_general x6, matrix products, contract(): lax.dot_general(left, right, (((left_dim,), (right_dim,)), ((), ())), pre...  27 us
  transfers between devices with their start and end apart: 4, of which 4 were waited for; matrix products, arithmetic and copies ran while one was open for 7% of the time, Pallas kernels for 0%

commit v1 on v0

--- a/solution.py
+++ b/solution.py
@@ -3,6 +3,11 @@
 import jax.numpy as jnp
 from jax import lax
 from jax.sharding import PartitionSpec as P
+
+
+def tiled_gather(x, axis, dim):
+    copies = jnp.concatenate([x] * lax.axis_size(axis), axis=dim)
+    return lax.all_to_all(copies, axis, dim, dim, tiled=True)
 
 
 def contract(left, right, left_dim, right_dim):
@@ -23,7 +28,7 @@
 def local(tokens, out_grad, gate_weight, up_weight, down_weight):
     panel_tokens, panel_grads = (
         lax.all_gather(tokens, "col", axis=0, tiled=True),
-        lax.all_gather(out_grad, "col", axis=0, tiled=True),
+        tiled_gather(out_grad, "col", 0),
     )
     factor = 1.0 / math.sqrt(panel_tokens.shape[0])
     gate_part = jnp.dot(panel_tokens, gate_weight, preferred_element_type=jnp.float32)

time: 327 us -> 294 us (0.90)
  waiting for transfers between devices: 270 us -> 185 us
  blocking collectives: 0 us -> 40 us
  local copies, waits for them, and re-layouts: 0.03 us -> 15 us
    all_gather x1, waiting for transfers between devices: 48.1 us -> 0.01 us  [local(): lax.all_gather(tokens, 'col', axis=0, tiled=True)]
    all_to_all x0 -> x1, blocking collectives: none -> 40 us  [tiled_gather(): return lax.all_to_all(copies, axis, dim, dim, tiled=True)]
    all_gather x1 -> x0, waiting for transfers between devices: 35.8 us -> none  [local(): lax.all_gather(out_grad, 'col', axis=0, tiled=True)]
    unnamed x16 -> x53, local copies, waits for them, and re-layouts: 0.03 us -> 15 us
  transfers between devices with their start and end apart: 4 -> 3, of which waited for: 4 -> 2; matrix products, arithmetic and copies ran while one was open for 7% -> 11% of each run, Pallas kernels for 0% -> 0%
where the time goes in v1:
time: 294 us; the launch traced here: 293 us
  waiting for transfers between devices  185 us (63%)
  blocking collectives  40 us (14%)
  matrix products  33.9 us (12%)
  local copies, waits for them, and re-layouts  15 us (5%)
  between operations  14 us (5%)
  other arithmetic  5.43 us (2%)
    psum x1, waiting for transfers between devices, local(): gate, upward, hid_grad = lax.psum((gate_part, up_part, grad_part), 'row')  116 us
    reduce_scatter x1, waiting for transfers between devices, local(): lax.psum_scatter(contract(gate_grad, gate_weight, 1, 1) + contract(up_gra...  68.2 us
    all_to_all x1, blocking collectives, tiled_gather(): return lax.all_to_all(copies, axis, dim, dim, tiled=True)  40 us
    dot_general x6, matrix products, contract(): lax.dot_general(left, right, (((left_dim,), (right_dim,)), ((), ())), pre...  24.3 us
    unnamed x53, local copies, waits for them, and re-layouts  15 us
    dot_general x1, matrix products, local(): jnp.dot(panel_tokens, up_weight, preferred_element_type=jnp.float32)  6.26 us
  transfers between devices with their start and end apart: 3, of which 2 were waited for; matrix products, arithmetic and copies ran while one was open for 11% of the time, Pallas kernels for 0%

profile of v1, /device:TPU:0, one launch (start us, length us, event | category | flops | bytes accessed | tf_op | source)
XLA Modules:
  0.0 293.3 jit_solution(10188254615536717915)
XLA Ops:
  7.2 0.0 copy-start
  7.2 0.0 all-gather.2.cloned.1.call-start
  7.2 0.7 all-gather.2.cloned.1.call-update
  7.9 0.0 all-reduce.3.cloned.1.call-start
  8.0 0.8 constant_dynamic-update-slice_fusion.31
  8.8 0.8 constant_dynamic-update-slice_fusion.30
  9.6 0.8 constant_dynamic-update-slice_fusion.29
  10.5 0.8 constant_dynamic-update-slice_fusion.28
  11.3 0.8 constant_dynamic-update-slice_fusion.27
  12.2 0.8 constant_dynamic-update-slice_fusion.26
  13.0 0.8 constant_dynamic-update-slice_fusion.25
  13.9 0.8 constant_dynamic-update-slice_fusion.24
  14.7 0.8 constant_dynamic-update-slice_fusion.23
  15.6 0.8 constant_dynamic-update-slice_fusion.22
  16.4 0.8 constant_dynamic-update-slice_fusion.21
  17.2 0.8 constant_dynamic-update-slice_fusion.20
  18.1 0.8 constant_dynamic-update-slice_fusion.19
  18.9 0.8 constant_dynamic-update-slice_fusion.18
  19.8 0.8 constant_dynamic-update-slice_fusion.17
  20.6 0.8 constant_dynamic-update-slice_fusion.16
  21.5 0.0 copy-done
  21.7 0.0 copy-start.8
  21.7 40.0 %all_to_all.12 = bf16[32,16,2048]{2,1,0:T(8,128)(2,1)S(1)} all-to-all(bf16[32,16,2048]{2,1,0:T(8,128)(2,1)S(1)} %bitcast.21), channel_id=1, replica_groups=mesh['row'=4,'col'=32] {'col'}, dimensions={0} | all-to-all | bytes 4194304 | tf_op jit(solution)/shard_map/all_to_all | solution.py:10
  61.7 0.0 copy-start.4
  61.7 1.3 copy-done.4
  63.1 0.0 copy-done.8
  63.1 3.4 %fusion.5 = f32[512,924]{0,1:T(8,128)} fusion(bf16[512,2048]{1,0:T(8,128)(2,1)S(1)} %bitcast.22, bf16[924,2048]{1,0:T(8,128)(2,1)S(1)} %copy-done.8), kind=kOutput, calls=%fused_computation.44 | convolution fusion | flops 1937768448 | bytes 7774208 | tf_op jit(solution)/shard_map/dot_general | solution.py:14
  66.5 0.0 all-gather.2.cloned.1.call-done
  66.5 0.0 copy-start.1
  66.5 0.0 copy-start.9
  66.5 6.3 %fusion.6 = f32[512,924]{0,1:T(8,128)} fusion(bf16[512,2048]{1,0:T(8,128)(2,1)} %all-gather.2.cloned.1.call-done, bf16[2048,924]{0,1:T(8,128)(2,1)} %param.8), kind=kOutput, calls=%fused_computation.45 | convolution fusion | flops 1937768448 | bytes 7774208 | tf_op jit(solution)/shard_map/dot_general | solution.py:35
  72.7 0.0 copy-done.1
  72.7 0.0 copy-done.9
  72.7 3.4 %fusion.7 = f32[512,924]{0,1:T(8,128)} fusion(bf16[512,2048]{1,0:T(8,128)(2,1)S(1)} %copy-done.9, bf16[2048,924]{0,1:T(8,128)(2,1)S(1)} %copy-done.1), kind=kOutput, calls=%fused_computation.46 | convolution fusion | flops 1937768448 | bytes 7774208 | tf_op jit(solution)/shard_map/dot_general | solution.py:34
  76.2 0.0 all-reduce.3.cloned.1.call-update
  76.2 0.2 reduce-scatter.2.cloned.1.call-start
  76.4 115.7 %all-reduce.3.cloned.1.call-done = (f32[512,924]{0,1:T(8,128)}, f32[512,924]{0,1:T(8,128)}, f32[512,924]{0,1:T(8,128)}) async-done(((f32[512,924]{0,1:T(8,128)}, f32[512,924]{0,1:T(8,128)}, f32[512,924]{0,1:T(8,128)}), (f32[512,924]{0,1:T(8,128)}, f32[512,924]{0,1:T(8,128)}, f32[512,924]{0,1:T(8,128)})) %all-reduce.3.cloned.1.call-update) | async-done | bytes 5677072 | tf_op jit(solution)/shard_map/psum | solution.py:37
  192.2 0.0 copy-start.2
  192.2 3.9 %multiply_convert_fusion.4 = (bf16[512,924]{0,1:T(8,128)(2,1)S(1)}, bf16[512,924]{0,1:T(8,128)(2,1)S(1)}) fusion(f32[512,924]{0,1:T(8,128)} %get-tuple-element.5, f32[512,924]{0,1:T(8,128)} %get-tuple-element.4, f32[512,924]{0,1:T(8,128)} %get-tuple-element.6), kind=kLoop, calls=%fused_computation.7 | loop fusion | flops 6150144 | bytes 7569408 | tf_op jit(solution)/shard_map/convert_element_type | solution.py:24
  196.1 0.0 copy-done.2
  196.1 0.0 copy-start.3
  196.1 2.4 fusion.8
  198.5 0.0 copy-done.3
  198.5 4.5 %convolution_add_fusion = f32[512,2048]{1,0:T(8,128)} fusion(f32[512,2048]{1,0:T(8,128)S(1)} %fusion.8, bf16[512,924]{0,1:T(8,128)(2,1)S(1)} %get-tuple-element.7, bf16[2048,924]{0,1:T(8,128)(2,1)S(1)} %copy-done.3), kind=kOutput, calls=%fused_computation.5 | convolution fusion | flops 1938817024 | bytes 13119488 | tf_op jit(solution)/shard_map/dot_general | solution.py:14
  203.0 0.0 reduce-scatter.2.cloned.1.call-update
  203.1 0.0 copy-start.10
  203.1 5.8 %fusion = bf16[2048,924]{0,1:T(8,128)(2,1)} fusion(bf16[512,924]{0,1:T(8,128)(2,1)S(1)} %get-tuple-element.8, bf16[512,2048]{1,0:T(8,128)(2,1)} %all-gather.2.cloned.1.call-done), kind=kOutput, calls=%fused_computation.3 | convolution fusion | flops 1941553152 | bytes 6828032 | tf_op jit(solution)/shard_map/dot_general | solution.py:14
  208.8 0.0 copy-done.10
  208.8 0.0 copy-start.5
  208.8 0.0 copy-start.6
  208.8 0.0 copy-start.7
  208.8 4.1 %fusion.1 = bf16[2048,924]{0,1:T(8,128)(2,1)} fusion(bf16[512,924]{0,1:T(8,128)(2,1)S(1)} %get-tuple-element.7, bf16[512,2048]{1,0:T(8,128)(2,1)S(1)} %copy-done.10), kind=kOutput, calls=%fused_computation.4 | convolution fusion | flops 1941553152 | bytes 6828032 | tf_op jit(solution)/shard_map/dot_general | solution.py:14
  212.9 0.0 copy-done.5
  212.9 0.0 copy-done.6
  212.9 0.0 copy-done.7
  212.9 4.1 %multiply_convert_fusion = bf16[924,2048]{1,0:T(8,128)(2,1)} fusion(bf16[512,2048]{1,0:T(8,128)(2,1)S(1)} %bitcast.23, f32[512,924]{0,1:T(8,128)S(1)} %copy-done.7, f32[512,924]{0,1:T(8,128)S(1)} %copy-done.6), kind=kOutput, calls=%fused_computation | convolution fusion | flops 1944391680 | bytes 9666560 | tf_op jit(solution)/shard_map/dot_general | solution.py:14
  217.0 68.2 %reduce-scatter.2.cloned.1.call-done = f32[16,2048]{1,0:T(8,128)} async-done(((f32[512,2048]{1,0:T(8,128)}), f32[16,2048]{1,0:T(8,128)}) %reduce-scatter.2.cloned.1.call-update) | async-done | bytes 131088 | tf_op jit(solution)/shard_map/reduce_scatter | solution.py:39
  285.2 1.5 convert_element_type.29
  (16 shorter events, 0.1 us)
Async XLA Ops:
  7.2 14.3 %copy-start = (bf16[16,2048]{1,0:T(8,128)(2,1)S(1)}, bf16[16,2048]{1,0:T(8,128)(2,1)}, u32[]{:S(2)}) copy-start(bf16[16,2048]{1,0:T(8,128)(2,1)} %param.6) | copy-start | bytes 196612
  7.2 59.3 %all-gather.2.cloned.1.call-start = ((), (), s32[]{:S(2)}) async-start(), calls=%async_computation.2 | async-start | bytes 2162688 | tf_op jit(solution)/shard_map/all_gather | solution.py:30
  7.9 184.2 %all-reduce.3.cloned.1.call-start = ((), (), s32[]{:S(2)}) async-start(), calls=%async_computation.4 | async-start | bytes 11403264 | tf_op jit(solution)/shard_map/psum | solution.py:37
  21.7 41.4 %copy-start.8 = (bf16[924,2048]{1,0:T(8,128)(2,1)S(1)}, bf16[924,2048]{1,0:T(8,128)(2,1)}, u32[]{:S(2)}) copy-start(bf16[924,2048]{1,0:T(8,128)(2,1)} %param.9) | copy-start | bytes 11354116
  61.7 1.3 copy-start.4
  66.5 6.3 %copy-start.1 = (bf16[2048,924]{0,1:T(8,128)(2,1)S(1)}, bf16[2048,924]{0,1:T(8,128)(2,1)}, u32[]{:S(2)}) copy-start(bf16[2048,924]{0,1:T(8,128)(2,1)} %param.7) | copy-start | bytes 11354116
  66.5 6.3 %copy-start.9 = (bf16[512,2048]{1,0:T(8,128)(2,1)S(1)}, bf16[512,2048]{1,0:T(8,128)(2,1)}, u32[]{:S(2)}) copy-start(bf16[512,2048]{1,0:T(8,128)(2,1)} %all-gather.2.cloned.1.call-done) | copy-start | bytes 6291460
  76.2 209.0 %reduce-scatter.2.cloned.1.call-start = ((), (), s32[]{:S(2)}) async-start(), calls=%async_computation.3 | async-start | bytes 4325376 | tf_op jit(solution)/shard_map/reduce_scatter | solution.py:39
  192.2 3.9 %copy-start.2 = (bf16[2048,924]{0,1:T(8,128)(2,1)S(1)}, bf16[2048,924]{0,1:T(8,128)(2,1)}, u32[]{:S(2)}) copy-start(bf16[2048,924]{0,1:T(8,128)(2,1)} %param.7) | copy-start | bytes 11354116
  196.1 2.4 copy-start.3
  203.1 5.8 %copy-start.10 = (bf16[512,2048]{1,0:T(8,128)(2,1)S(1)}, bf16[512,2048]{1,0:T(8,128)(2,1)}, u32[]{:S(2)}) copy-start(bf16[512,2048]{1,0:T(8,128)(2,1)} %all-gather.2.cloned.1.call-done) | copy-start | bytes 6291460
  208.8 4.1 %copy-start.5 = (bf16[32,16,2048]{2,1,0:T(8,128)(2,1)S(1)}, bf16[32,16,2048]{2,1,0:T(8,128)(2,1)}, u32[]{:S(2)}) copy-start(bf16[32,16,2048]{2,1,0:T(8,128)(2,1)} %copy-done.4) | copy-start | bytes 6291460
  208.8 4.1 %copy-start.6 = (f32[512,924]{0,1:T(8,128)S(1)}, f32[512,924]{0,1:T(8,128)}, u32[]{:S(2)}) copy-start(f32[512,924]{0,1:T(8,128)} %get-tuple-element.4) | copy-start | bytes 5677060
  208.8 4.1 %copy-start.7 = (f32[512,924]{0,1:T(8,128)S(1)}, f32[512,924]{0,1:T(8,128)}, u32[]{:S(2)}) copy-start(f32[512,924]{0,1:T(8,128)} %get-tuple-element.6) | copy-start | bytes 5677060
Sparse Core Ops, SparseCore 0:
  10.3 55.3 all-gather.1
  76.3 115.8 all-reduce.2
  203.2 81.9 reduce-scatter.1
